TPU v7x, 32 devices: a whole 2x2x4 slice. The times are simulated.
32 devices in a mesh: dp: 16 (over z, y, x), rep: 2 (over core).
Axes of the slice: x: 2, y: 2, z: 4, core: 2. Of those that a mesh axis runs over, the one named last changes fastest.
Arguments:
- features: bfloat16 [4096, 1024], P(('dp', 'rep')), may hold values from -6 to 6
- cotangent: bfloat16 [4096, 1024], P(('dp', 'rep')), may hold values from -6 to 6
- routes: int32 [4096, 2], P(('dp', 'rep')), may hold values from 0 to 15, all different within a row; in each aligned block of 128 rows (0 to 127, 128 to 255, ...) at most 24 rows name the same one
- route_weights: float32 [4096, 2], P(('dp', 'rep')), may hold values from 0.2 to 1
- counts: int32 [4096], P(('dp', 'rep')), may hold values from 1 to 4
- cross_weight: bfloat16 [1024, 1024], P(('dp', 'rep')), may hold values from -0.1875 to 0.1875
- gate_weight: bfloat16 [1024, 1024], P(('dp', 'rep')), may hold values from -0.1875 to 0.1875
- cross_bias: float32 [1024], replicated, may hold values from -3 to 3
- gate_bias: float32 [1024], replicated, may hold values from -4 to 4
- expert_in: bfloat16 [16, 1024, 2048], P('dp', None, 'rep'), may hold values from -0.1875 to 0.1875
- expert_out: bfloat16 [16, 2048, 1024], P('dp', 'rep'), may hold values from -0.125 to 0.125
Outputs:
- layer_output: bfloat16 [4096, 1024], P(('dp', 'rep'))
- grad_cross_weight: bfloat16 [1024, 1024], P('rep')
- grad_gate_weight: bfloat16 [1024, 1024], P('rep')
- grad_cross_bias: float32 [1024], P('rep')
- grad_gate_bias: float32 [1024], P('rep')
- grad_expert_in: bfloat16 [16, 1024, 2048], P('dp', None, 'rep')
- grad_expert_out: bfloat16 [16, 2048, 1024], P('dp', 'rep')
Inputs may be any that keep to these rules, and one draw needn't show every extreme that they name: `routes`: the two experts of a row differ. In the rows of one device (aligned blocks of 128 rows) no expert is named more than 24 times, and in every draw some expert is named exactly 24 times in some block. Every expert is named by some row.
All inputs are finite; a program needn't handle non-finite values.
Results may differ from a plain program's by a relative error of at most 0.02.
Values may be sent and summed in bfloat16 or wider, within the bound.
A program may use at most 128 MiB of HBM per device.

v0:
```python
import jax
import jax.numpy as jnp
from jax import lax
from jax.sharding import PartitionSpec as P


def slot_layout(routes, experts_n, capacity):
    flat_routes = routes.reshape(-1)
    onehot = (flat_routes[:, None] == jnp.arange(experts_n, dtype=jnp.int32)[None, :]).astype(
        jnp.int32
    )
    position = jnp.sum((jnp.cumsum(onehot, axis=0) - 1) * onehot, axis=1)
    slot_index = flat_routes * capacity + position
    slot_ids = jnp.arange(experts_n * capacity, dtype=jnp.int32)
    slot_match = (slot_index[None, :] == slot_ids[:, None]).astype(jnp.bfloat16)
    return (slot_index, slot_match)


def body(
    features,
    cotangent,
    routes,
    route_weights,
    counts,
    cross_weight,
    gate_weight,
    cross_bias,
    gate_bias,
    expert_in,
    expert_out,
):
    row_count, width = features.shape
    experts_n = lax.axis_size("dp")
    capacity = max(2, 3 * row_count // experts_n)
    feature_f = features.astype(jnp.float32)
    cross_acc = jnp.dot(
        features,
        lax.all_gather(cross_weight, ("dp", "rep"), axis=0, tiled=True),
        preferred_element_type=jnp.float32,
    )
    gate_acc = jnp.dot(
        features,
        lax.all_gather(gate_weight, ("dp", "rep"), axis=0, tiled=True),
        preferred_element_type=jnp.float32,
    )
    cross_term = cross_acc + cross_bias
    gate_term = jax.nn.sigmoid(gate_acc + gate_bias)
    crossed = (feature_f * cross_term * gate_term + feature_f).astype(jnp.bfloat16)
    slot_index, slot_match = slot_layout(routes, experts_n, capacity)
    row_match = jnp.sum(slot_match.reshape(experts_n * capacity, row_count, 2), axis=2)
    send_buffer = jnp.dot(row_match, crossed, preferred_element_type=jnp.float32).astype(
        jnp.bfloat16
    )
    send_buffer = send_buffer.reshape(experts_n, capacity, width)
    weight_in = expert_in[0]
    weight_out = expert_out[0]
    rows_all = lax.all_gather(
        lax.all_to_all(send_buffer, "dp", split_axis=0, concat_axis=0, tiled=True),
        "rep",
        axis=0,
        tiled=True,
    )
    pre_act = jnp.einsum("skd,df->skf", rows_all, weight_in, preferred_element_type=jnp.float32)
    hidden = (pre_act * jax.nn.sigmoid(pre_act)).astype(jnp.bfloat16)
    partial_value = jnp.einsum(
        "skf,fd->skd", hidden, weight_out, preferred_element_type=jnp.float32
    )
    result = lax.psum_scatter(
        partial_value.astype(jnp.bfloat16), "rep", scatter_dimension=0, tiled=True
    )
    expert_result, slot_inputs, pre_act, hidden = (result, rows_all, pre_act, hidden)
    returned = lax.all_to_all(expert_result, "dp", split_axis=0, concat_axis=0, tiled=True)
    gathered_out = (
        returned.reshape(experts_n * capacity, width)[slot_index]
        .reshape(row_count, 2, width)
        .astype(jnp.float32)
    )
    layer_output = (
        crossed.astype(jnp.float32) + jnp.sum(route_weights[:, :, None] * gathered_out, axis=1)
    ).astype(jnp.bfloat16)
    upstream = 0.05 * counts.astype(jnp.float32)[:, None] * cotangent.astype(jnp.float32)
    out_grad = (
        (route_weights[:, :, None] * upstream[:, None, :])
        .astype(jnp.bfloat16)
        .reshape(2 * row_count, width)
    )
    grad_send = jnp.dot(slot_match, out_grad, preferred_element_type=jnp.float32).astype(
        jnp.bfloat16
    )
    grad_send = grad_send.reshape(experts_n, capacity, width)
    grad_recv = lax.all_to_all(grad_send, "dp", split_axis=0, concat_axis=0, tiled=True)
    squash = jax.nn.sigmoid(pre_act)
    slope = squash * (1.0 + pre_act * (1.0 - squash))
    slot_grads = lax.all_gather(grad_recv, "rep", axis=0, tiled=True)
    hid_grad = jnp.einsum("skd,fd->skf", slot_grads, weight_out, preferred_element_type=jnp.float32)
    pre_grad = (hid_grad * slope).astype(jnp.bfloat16)
    back_part = jnp.einsum("skf,df->skd", pre_grad, weight_in, preferred_element_type=jnp.float32)
    back_rows = lax.psum_scatter(
        back_part.astype(jnp.bfloat16), "rep", scatter_dimension=0, tiled=True
    )
    returned_grad = lax.all_to_all(back_rows, "dp", split_axis=0, concat_axis=0, tiled=True)
    grad_in_full = jnp.einsum(
        "skd,skf->df", slot_inputs, pre_grad, preferred_element_type=jnp.float32
    )
    grad_out_full = jnp.einsum(
        "skf,skd->fd", hidden, slot_grads, preferred_element_type=jnp.float32
    )
    grad_in_part = grad_in_full[None]
    grad_out_part = grad_out_full[None]
    grad_expert_in = grad_in_part.astype(jnp.bfloat16)
    grad_expert_out = grad_out_part.astype(jnp.bfloat16)
    back_gathered = (
        returned_grad.reshape(experts_n * capacity, width)[slot_index]
        .reshape(row_count, 2, width)
        .astype(jnp.float32)
    )
    crossed_grad = upstream + jnp.sum(back_gathered, axis=1)
    cross_grad = (crossed_grad * feature_f * gate_term).astype(jnp.bfloat16)
    gate_grad = (crossed_grad * feature_f * cross_term * gate_term * (1.0 - gate_term)).astype(
        jnp.bfloat16
    )
    weight_cross = jnp.einsum("rd,re->de", features, cross_grad, preferred_element_type=jnp.float32)
    weight_gate = jnp.einsum("rd,re->de", features, gate_grad, preferred_element_type=jnp.float32)
    bias_cross = jnp.sum(cross_grad.astype(jnp.float32), axis=0)
    bias_gate = jnp.sum(gate_grad.astype(jnp.float32), axis=0)
    halves = (
        lax.psum_scatter(
            weight_cross.astype(jnp.bfloat16), "rep", scatter_dimension=0, tiled=True
        ).astype(jnp.float32),
        lax.psum_scatter(
            weight_gate.astype(jnp.bfloat16), "rep", scatter_dimension=0, tiled=True
        ).astype(jnp.float32),
        lax.psum_scatter(
            bias_cross.astype(jnp.bfloat16), "rep", scatter_dimension=0, tiled=True
        ).astype(jnp.float32),
        lax.psum_scatter(
            bias_gate.astype(jnp.bfloat16), "rep", scatter_dimension=0, tiled=True
        ).astype(jnp.float32),
    )
    summed = lax.psum((halves[0], halves[1], halves[2], halves[3]), "dp")
    return (
        layer_output,
        summed[0].astype(jnp.bfloat16),
        summed[1].astype(jnp.bfloat16),
        summed[2],
        summed[3],
        grad_expert_in,
        grad_expert_out,
    )


def solution(mesh):
    return jax.shard_map(
        body,
        mesh=mesh,
        in_specs=(
            P(("dp", "rep"), None),
            P(("dp", "rep"), None),
            P(("dp", "rep"), None),
            P(("dp", "rep"), None),
            P(("dp", "rep")),
            P(("dp", "rep"), None),
            P(("dp", "rep"), None),
            P(),
            P(),
            P("dp", None, "rep"),
            P("dp", "rep", None),
        ),
        out_specs=(
            P(("dp", "rep"), None),
            P("rep", None),
            P("rep", None),
            P("rep"),
            P("rep"),
            P("dp", None, "rep"),
            P("dp", "rep", None),
        ),
        check_vma=False,
    )
```

profile of v0, /device:TPU:0, one launch (start us, length us, event | category | flops | bytes accessed | tf_op | source)
XLA Modules:
  0.0 414.2 jit_solution(13972650202098008798)
XLA Ops:
  7.2 0.7 all-gather.5.cloned.1.call-update
  8.0 0.7 all-gather.7.cloned.1.call-update
  8.7 0.8 copy.47
  9.5 0.1 eq.45
  9.6 0.1 eq.49
  9.8 0.6 reduce-window.6
  10.4 0.2 slice_reduce_fusion
  10.6 0.1 fusion.29
  10.7 0.1 reduce_sum.68
  10.9 0.1 copy.51
  10.9 0.1 fusion.26
  11.0 59.0 %all-gather.5.cloned.1.call-done = bf16[1024,1024]{1,0:T(8,128)(2,1)} async-done(((bf16[32,1024]{1,0:T(8,128)(2,1)}), bf16[1024,1024]{1,0:T(8,128)(2,1)}) %all-gather.5.cloned.1.call-update) | async-done | bytes 2097168 | tf_op jit(solution)/shard_map/all_gather | solution.py:38
  70.0 2.0 convolution_add_fusion.1
  72.1 56.1 %all-gather.7.cloned.1.call-done = bf16[1024,1024]{1,0:T(8,128)(2,1)} async-done(((bf16[32,1024]{1,0:T(8,128)(2,1)}), bf16[1024,1024]{1,0:T(8,128)(2,1)}) %all-gather.7.cloned.1.call-update) | async-done | bytes 2097168 | tf_op jit(solution)/shard_map/all_gather | solution.py:43
  128.1 2.9 fusion.23
  131.1 0.7 copy-done.5
  131.7 1.2 convolution_convert_fusion.1
  133.0 4.5 %all-to-all-start = ((bf16[16,24,1024]{2,1,0:T(8,128)(2,1)}), bf16[16,24,1024]{2,1,0:T(8,128)(2,1)}, u32[]{:S(2)}, u32[]{:S(2)}) async-start(bf16[16,24,1024]{2,1,0:T(8,128)(2,1)} %bitcast.1), calls=%async_computation | async-start | bytes 1572864 | tf_op jit(solution)/shard_map/all_to_all | solution.py:58
  137.5 0.0 all-gather.9.cloned.1.call-start
  137.6 0.1 copy.46
  137.7 0.1 mul.118
  137.9 0.1 convert_multiply_fusion.2
  138.0 0.4 copy-done.7
  138.4 1.3 mul.120
  139.7 1.9 mul.121
  141.6 16.0 %all-to-all-done = bf16[16,24,1024]{2,1,0:T(8,128)(2,1)} async-done(((bf16[16,24,1024]{2,1,0:T(8,128)(2,1)}), bf16[16,24,1024]{2,1,0:T(8,128)(2,1)}, u32[]{:S(2)}, u32[]{:S(2)}) %all-to-all-start) | async-done | bytes 786464 | tf_op jit(solution)/shard_map/all_to_all | solution.py:58
  157.6 0.0 all-gather.11.cloned.1.call-start
  157.7 0.5 convolution_convert_fusion
  158.2 25.2 %all_to_all.20 = bf16[16,24,1024]{2,1,0:T(8,128)(2,1)} all-to-all(bf16[16,24,1024]{2,1,0:T(8,128)(2,1)S(1)} %bitcast.74), channel_id=1, replica_groups=mesh['dp'=16,'rep'=2] {'dp'}, dimensions={0} | all-to-all | bytes 1572864 | tf_op jit(solution)/shard_map/all_to_all | solution.py:91
  183.4 0.0 reduce-scatter.7.cloned.1.call-start
  183.5 4.9 %fusion.6 = f32[32,24,1024]{2,1,0:T(8,128)} fusion(bf16[32,24,1024]{2,1,0:T(8,128)(2,1)} %all-gather.9.cloned.1.call-done, bf16[1,1024,1024]{2,1,0:T(8,128)(2,1)S(1)} %copy-done), kind=kOutput, calls=%fused_computation.13 | convolution fusion | flops 1610612736 | bytes 6815744 | tf_op jit(solution)/shard_map/skd,df->skf/dot_general | solution.py:63
  188.4 2.8 all-gather.11.cloned.1.call-done
  191.1 5.4 %multiply_convert_fusion = bf16[32,24,1024]{2,1,0:T(8,128)(2,1)S(1)} fusion(f32[32,24,1024]{2,1,0:T(8,128)} %fusion.6, bf16[32,24,1024]{2,1,0:T(8,128)(2,1)} %all-gather.11.cloned.1.call-done, bf16[1,1024,1024]{2,1,0:T(8,128)(2,1)} %param.21), kind=kOutput, calls=%fused_computation.4 | convolution fusion | flops 1617690624 | bytes 8388608 | tf_op jit(solution)/shard_map/skd,fd->skf/dot_general | solution.py:95
  196.5 1.2 copy-done.13
  197.7 3.0 fusion.8
  200.7 5.7 %fusion.11 = bf16[32,24,1024]{2,1,0:T(8,128)(2,1)} fusion(bf16[1,1024,1024]{2,1,0:T(8,128)(2,1)} %param.21, f32[32,24,1024]{2,1,0:T(8,128)} %fusion.6), kind=kOutput, calls=%fused_computation.18 | convolution fusion | flops 1615331328 | bytes 6815744 | tf_op jit(solution)/shard_map/skf,fd->skd/dot_general | solution.py:65
  206.5 4.6 %reduce-scatter.7.cloned.1.call-done = bf16[16,24,1024]{2,1,0:T(8,128)(2,1)} async-done(((bf16[32,24,1024]{2,1,0:T(8,128)(2,1)}), bf16[16,24,1024]{2,1,0:T(8,128)(2,1)}) %reduce-scatter.7.cloned.1.call-update) | async-done | bytes 786448 | tf_op jit(solution)/shard_map/reduce_scatter | solution.py:98
  211.0 6.8 %all-to-all-start.3 = ((bf16[16,24,1024]{2,1,0:T(8,128)(2,1)}), bf16[16,24,1024]{2,1,0:T(8,128)(2,1)S(1)}, u32[]{:S(2)}, u32[]{:S(2)}) async-start(bf16[16,24,1024]{2,1,0:T(8,128)(2,1)} %reduce-scatter.7.cloned.1.call-done), calls=%async_computation.5 | async-start | bytes 1572864 | tf_op jit(solution)/shard_map/all_to_all | solution.py:101
  217.9 0.2 reduce-scatter.11.cloned.1.call-start
  218.1 0.1 mul.110
  218.2 19.7 %all-to-all-done.3 = bf16[16,24,1024]{2,1,0:T(8,128)(2,1)S(1)} async-done(((bf16[16,24,1024]{2,1,0:T(8,128)(2,1)}), bf16[16,24,1024]{2,1,0:T(8,128)(2,1)S(1)}, u32[]{:S(2)}, u32[]{:S(2)}) %all-to-all-start.3) | async-done | bytes 786464 | tf_op jit(solution)/shard_map/all_to_all | solution.py:101
  237.9 2.0 gather_fusion.1
  239.9 1.7 reshape.115
  241.6 2.1 reduce_sum.72
  243.7 1.8 fusion.32
  245.5 2.1 convert_bitcast_fusion
  247.6 2.1 convert_bitcast_fusion.1
  249.7 0.6 dynamic-slice
  251.0 5.9 %fusion.15 = bf16[1,1024,1024]{2,1,0:T(8,128)(2,1)} fusion(bf16[32,24,1024]{2,1,0:T(8,128)(2,1)} %all-gather.11.cloned.1.call-done, f32[32,24,1024]{2,1,0:T(8,128)} %fusion.6), kind=kOutput, calls=%fused_computation.20 | convolution fusion | flops 1615593472 | bytes 6815744 | tf_op jit(solution)/shard_map/skf,skd->fd/dot_general | solution.py:105
  256.9 4.7 %all-to-all-start.1 = ((bf16[16,24,1024]{2,1,0:T(8,128)(2,1)}), bf16[16,24,1024]{2,1,0:T(8,128)(2,1)S(1)}, u32[]{:S(2)}, u32[]{:S(2)}) async-start(bf16[16,24,1024]{2,1,0:T(8,128)(2,1)} %reduce-scatter.5.cloned.1.call-done), calls=%async_computation.2 | async-start | bytes 1572864 | tf_op jit(solution)/shard_map/all_to_all | solution.py:72
  261.5 0.0 all-reduce.7.cloned.1.call-start
  261.6 8.8 %reduce-scatter.9.cloned.1.call-done = bf16[512,1024]{0,1:T(8,128)(2,1)} async-done(((bf16[1024,1024]{0,1:T(8,128)(2,1)}), bf16[512,1024]{0,1:T(8,128)(2,1)}) %reduce-scatter.9.cloned.1.call-update) | async-done | bytes 1048592 | tf_op jit(solution)/shard_map/reduce_scatter | solution.py:127
  270.5 5.0 %fusion.14 = bf16[1,1024,1024]{2,1,0:T(8,128)(2,1)} fusion(bf16[32,24,1024]{2,1,0:T(8,128)(2,1)} %all-gather.9.cloned.1.call-done, bf16[32,24,1024]{2,1,0:T(8,128)(2,1)} %copy-done.13), kind=kOutput, calls=%fused_computation.19 | convolution fusion | flops 1611661312 | bytes 5242880 | tf_op jit(solution)/shard_map/skd,skf->df/dot_general | solution.py:102
  275.5 4.8 %all-to-all-done.1 = bf16[16,24,1024]{2,1,0:T(8,128)(2,1)S(1)} async-done(((bf16[16,24,1024]{2,1,0:T(8,128)(2,1)}), bf16[16,24,1024]{2,1,0:T(8,128)(2,1)S(1)}, u32[]{:S(2)}, u32[]{:S(2)}) %all-to-all-start.1) | async-done | bytes 786464 | tf_op jit(solution)/shard_map/all_to_all | solution.py:72
  280.3 2.0 gather_fusion
  282.3 1.8 reshape.114
  284.1 2.5 all-reduce.4
  286.6 0.1 dynamic-slice_convert_fusion
  286.7 41.3 %all-reduce.2 = (f32[512]{0:T(512)}, f32[512]{0:T(512)}) all-reduce(f32[512]{0:T(512)S(1)} %get-tuple-element.52, f32[512]{0:T(512)S(1)} %get-tuple-element.51), channel_id=1, replica_groups=mesh['dp'=16,'rep'=2] {'dp'}, use_global_device_ids=true, to_apply=%region_14.15 | all-reduce | flops 1024 | bytes 8192 | tf_op jit(solution)/shard_map/psum | solution.py:140
  327.9 1.3 multiply_reduce_fusion
  329.3 0.8 add_convert_fusion
  330.1 73.9 %all-reduce.7.cloned.1.call-done = (bf16[512,1024]{0,1:T(8,128)(2,1)}, bf16[512,1024]{0,1:T(8,128)(2,1)}) async-done(((bf16[512,1024]{0,1:T(8,128)(2,1)}, bf16[512,1024]{0,1:T(8,128)(2,1)}), (bf16[512,1024]{0,1:T(8,128)(2,1)}, bf16[512,1024]{0,1:T(8,128)(2,1)})) %all-reduce.7.cloned.1.call-update) | async-done | bytes 2097168 | tf_op jit(solution)/shard_map/psum | solution.py:140
  404.0 2.4 copy.53
  406.3 1.3 copy.54
  (47 shorter events, 0.5 us)
Async XLA Ops:
  7.2 176.3 %copy-start = (bf16[1,1024,1024]{2,1,0:T(8,128)(2,1)S(1)}, bf16[1,1024,1024]{2,1,0:T(8,128)(2,1)}, u32[]{:S(2)}) copy-start(bf16[1,1024,1024]{2,1,0:T(8,128)(2,1)} %param.20) | copy-start | bytes 6291460
  7.2 120.9 %copy-start.1 = (bf16[128,1024]{1,0:T(8,128)(2,1)S(1)}, bf16[128,1024]{1,0:T(8,128)(2,1)}, u32[]{:S(2)}) copy-start(bf16[128,1024]{1,0:T(8,128)(2,1)} %param.11) | copy-start | bytes 786436
  7.2 120.9 %copy-start.10 = (f32[1024]{0:T(1024)S(1)}, f32[1024]{0:T(1024)}, u32[]{:S(2)}) copy-start(f32[1024]{0:T(1024)} %param.19) | copy-start | bytes 12292
  7.2 62.8 %all-gather.5.cloned.1.call-start = ((), (), s32[]{:S(2)}) async-start(), calls=%async_computation.8 | async-start | bytes 2162688 | tf_op jit(solution)/shard_map/all_gather | solution.py:38
  7.9 120.2 %all-gather.7.cloned.1.call-start = ((), (), s32[]{:S(2)}) async-start(), calls=%async_computation.9 | async-start | bytes 2162688 | tf_op jit(solution)/shard_map/all_gather | solution.py:43
  72.0 59.0 %copy-start.2 = (f32[128,1024]{1,0:T(8,128)}, f32[128,1024]{1,0:T(8,128)S(1)}, u32[]{:S(2)}) copy-start(f32[128,1024]{1,0:T(8,128)S(1)} %convolution_add_fusion.1) | copy-start | bytes 1572868
  131.0 0.7 copy-start.5
  131.0 6.5 %copy-start.9 = (f32[128,2]{0,1:T(2,128)S(1)}, f32[128,2]{0,1:T(2,128)}, u32[]{:S(2)}) copy-start(f32[128,2]{0,1:T(2,128)} %param.14) | copy-start | bytes 3076
  131.0 6.8 %copy-start.11 = (s32[128]{0:T(128)S(1)}, s32[128]{0:T(128)}, u32[]{:S(2)}) copy-start(s32[128]{0:T(128)} %param.15) | copy-start | bytes 1540
  131.0 6.8 %copy-start.4 = (bf16[128,1024]{1,0:T(8,128)(2,1)S(1)}, bf16[128,1024]{1,0:T(8,128)(2,1)}, u32[]{:S(2)}) copy-start(bf16[128,1024]{1,0:T(8,128)(2,1)} %param.12) | copy-start | bytes 786436
  133.0 24.6 %all-to-all-start = ((bf16[16,24,1024]{2,1,0:T(8,128)(2,1)}), bf16[16,24,1024]{2,1,0:T(8,128)(2,1)}, u32[]{:S(2)}, u32[]{:S(2)}) async-start(bf16[16,24,1024]{2,1,0:T(8,128)(2,1)} %bitcast.1), calls=%async_computation | async-start | bytes 1572864 | tf_op jit(solution)/shard_map/all_to_all | solution.py:58
  137.5 46.0 %all-gather.9.cloned.1.call-start = ((), (), s32[]{:S(2)}) async-start(), calls=%async_computation.10 | async-start | bytes 2359296 | tf_op jit(solution)/shard_map/all_gather | solution.py:57
  137.8 0.5 copy-start.7
  157.6 33.5 %all-gather.11.cloned.1.call-start = ((), (), s32[]{:S(2)}) async-start(), calls=%async_computation.12 | async-start | bytes 2359296 | tf_op jit(solution)/shard_map/all_gather | solution.py:94
  183.4 27.6 %reduce-scatter.7.cloned.1.call-start = ((), (), s32[]{:S(2)}) async-start(), calls=%async_computation.13 | async-start | bytes 2359296 | tf_op jit(solution)/shard_map/reduce_scatter | solution.py:98
  196.5 1.2 copy-start.13
  200.7 56.2 %reduce-scatter.5.cloned.1.call-start = ((), (), s32[]{:S(2)}) async-start(), calls=%async_computation.11 | async-start | bytes 2359296 | tf_op jit(solution)/shard_map/reduce_scatter | solution.py:68
  211.0 26.9 %all-to-all-start.3 = ((bf16[16,24,1024]{2,1,0:T(8,128)(2,1)}), bf16[16,24,1024]{2,1,0:T(8,128)(2,1)S(1)}, u32[]{:S(2)}, u32[]{:S(2)}) async-start(bf16[16,24,1024]{2,1,0:T(8,128)(2,1)} %reduce-scatter.7.cloned.1.call-done), calls=%async_computation.5 | async-start | bytes 1572864 | tf_op jit(solution)/shard_map/all_to_all | solution.py:101
  217.9 43.8 %reduce-scatter.11.cloned.1.call-start = ((), (), s32[]{:S(2)}) async-start(), calls=%async_computation.15 | async-start | bytes 3145728 | tf_op jit(solution)/shard_map/reduce_scatter | solution.py:130
  239.9 3.8 copy-start.8
  247.6 22.9 %reduce-scatter.9.cloned.1.call-start = ((), (), s32[]{:S(2)}) async-start(), calls=%async_computation.14 | async-start | bytes 3145728 | tf_op jit(solution)/shard_map/reduce_scatter | solution.py:127
  247.6 2.1 copy-start.12
  256.9 23.4 %all-to-all-start.1 = ((bf16[16,24,1024]{2,1,0:T(8,128)(2,1)}), bf16[16,24,1024]{2,1,0:T(8,128)(2,1)S(1)}, u32[]{:S(2)}, u32[]{:S(2)}) async-start(bf16[16,24,1024]{2,1,0:T(8,128)(2,1)} %reduce-scatter.5.cloned.1.call-done), calls=%async_computation.2 | async-start | bytes 1572864 | tf_op jit(solution)/shard_map/all_to_all | solution.py:72
  261.5 142.4 %all-reduce.7.cloned.1.call-start = ((), (), s32[]{:S(2)}) async-start(), calls=%async_computation.16 | async-start | bytes 4194304 | tf_op jit(solution)/shard_map/psum | solution.py:140
  282.2 47.0 %copy-start.6 = (bf16[128,1024]{1,0:T(8,128)(2,1)S(1)}, bf16[128,1024]{1,0:T(8,128)(2,1)}, u32[]{:S(2)}) copy-start(bf16[128,1024]{1,0:T(8,128)(2,1)} %copy-done.5) | copy-start | bytes 786436
  404.0 2.4 copy-start.3
Sparse Core Ops, SparseCore 0:
  10.9 59.0 all-gather.4
  72.9 55.2 all-gather.6
  157.8 9.2 all-gather.8
  183.5 7.5 all-gather.10
  200.8 10.1 reduce-scatter.6
  213.2 10.2 reduce-scatter.4
  247.7 8.9 reduce-scatter.10
  259.6 10.7 reduce-scatter.8
  276.0 127.9 all-reduce.6
where the time goes:
time: 415 us; the launch traced here: 414 us
  waiting for transfers between devices  247 us (60%)
  blocking collectives  69 us (17%)
  matrix products  40.6 us (10%)
  local copies, waits for them, and re-layouts  19.1 us (5%)
  starting transfers between devices  16.6 us (4%)
  between operations  14.8 us (4%)
  other arithmetic  7.01 us (2%)
    psum x1, waiting for transfers between devices, body(): summed = lax.psum((halves[0], halves[1], halves[2], halves[3]), 'dp')  73.9 us
    all_gather x1, waiting for transfers between devices, body(): lax.all_gather(cross_weight, ('dp', 'rep'), axis=0, tiled=True)  59 us
    all_gather x1, waiting for transfers between devices, body(): lax.all_gather(gate_weight, ('dp', 'rep'), axis=0, tiled=True)  56.1 us
    psum x1, blocking collectives, body(): summed = lax.psum((halves[0], halves[1], halves[2], halves[3]), 'dp')  41.3 us
    all_to_all x1, blocking collectives, body(): lax.all_to_all(grad_send, 'dp', split_axis=0, concat_axis=0, tiled=True)  25.2 us
    all_to_all x1, waiting for transfers between devices, body(): lax.all_to_all(back_rows, 'dp', split_axis=0, concat_axis=0, tiled=True)  19.7 us
    all_to_all x1, waiting for transfers between devices, body(): lax.all_to_all(send_buffer, 'dp', split_axis=0, concat_axis=0, tiled=True)  16 us
    reduce_scatter x1, waiting for transfers between devices, body(): lax.psum_scatter(weight_cross.astype(jnp.bfloat16), 'rep', scatter_dimens...  8.84 us
  transfers between devices with their start and end apart: 12, of which 9 were waited for; matrix products, arithmetic and copies ran while one was open for 12% of the time, Pallas kernels for 0%

commit v1 on v0

v1 whole, which is shorter than its diff:
```python
import functools

import jax
import jax.numpy as jnp
from jax import lax
from jax.experimental import pallas as pl
from jax.experimental.pallas import tpu as pltpu
from jax.sharding import PartitionSpec as P

MESH = pl.DeviceIdType.MESH
DMA = pltpu.SemaphoreType.DMA


def flip(index, mask):
    bit = 1
    while bit <= mask:
        if mask & bit:
            index = index + bit * (1 - 2 * ((index // bit) % 2))
        bit *= 2
    return index


def bit_orders(n):
    bits = n.bit_length() - 1
    down = list(range(bits))[::-1]
    turned = down[:1] + down[2:] + down[1:2]
    return down, turned


def greet(me, rep, partners, everyone=0):
    barrier = pltpu.get_barrier_semaphore()
    pl.semaphore_signal(barrier, inc=1, device_id=(me, 1 - rep), device_id_type=MESH)
    count = 1
    if everyone:
        for d in range(1, everyone):
            to = lax.rem(me + d, everyone)
            pl.semaphore_signal(barrier, inc=1, device_id=(to, rep), device_id_type=MESH)
            count += 1
    else:
        for mask in partners:
            pl.semaphore_signal(
                barrier, inc=1, device_id=(flip(me, mask), rep), device_id_type=MESH
            )
            count += 1
    pl.semaphore_wait(barrier, count)


def remote(src, dst, send, recv, to):
    return pltpu.make_async_remote_copy(
        src_ref=src, dst_ref=dst, send_sem=send, recv_sem=recv, device_id=to, device_id_type=MESH
    )


class Spread:
    def __init__(self, n, me, rep, src, dst, sems):
        self.n, self.me, self.rep = n, me, rep
        self.src, self.dst = src, dst
        self.send, self.recv, self.sib_send, self.sib_recv, self.local = sems
        self.started = []

    def start_own(self):
        n, me, rep = self.n, self.me, self.rep
        copy = pltpu.make_async_copy(self.src.at[me], self.dst.at[rep, me], self.local.at[0])
        copy.start()
        self.own = copy
        sib = remote(
            self.src.at[me], self.dst.at[rep, me], self.sib_send.at[0], self.sib_recv.at[0],
            (me, 1 - rep),
        )
        sib.start()
        self.started.append(sib)

    def start_to(self, d):
        n, me, rep = self.n, self.me, self.rep
        to = lax.rem(me + d, n)
        copy = remote(
            self.src.at[to], self.dst.at[rep, me], self.send.at[d], self.recv.at[d], (to, rep)
        )
        copy.start()
        self.started.append(copy)

    def pass_on(self, d):
        n, me, rep = self.n, self.me, self.rep
        origin = lax.rem(me + (n - d), n)
        block = self.dst.at[rep, origin]
        remote(block, block, self.send.at[d], self.recv.at[d], (me, 1 - rep)).wait_recv()
        copy = remote(
            block, block, self.sib_send.at[d], self.sib_recv.at[d], (me, 1 - rep)
        )
        copy.start()
        self.started.append(copy)

    def finish(self):
        n, me, rep = self.n, self.me, self.rep
        self.own.wait()
        for d in range(n):
            block = self.dst.at[1 - rep, lax.rem(me + (n - d), n)]
            remote(
                block, block, self.sib_send.at[d], self.sib_recv.at[d], (me, 1 - rep)
            ).wait_recv()
        for copy in self.started:
            copy.wait_send()


def order_of(n):
    return list(range(1, n))


def gather_kernel(n, cross_ref, gate_ref, grads_ref, cross_full, gate_full, slots, *sems):
    me, rep = lax.axis_index("dp"), lax.axis_index("rep")
    greet(me, rep, (), n)
    spread = Spread(n, me, rep, grads_ref, slots, sems[5:])
    ag_send, ag_recv, sib_send, sib_recv, own = sems[:5]
    sources, fulls, orders = (cross_ref, gate_ref), (cross_full, gate_full), bit_orders(n)
    started, waits = [], []

    def to_sibling(a, mask):
        place = fulls[a].at[flip(me, mask), rep]
        copy = remote(
            sources[a] if mask == 0 else place, place, sib_send.at[a, mask], sib_recv.at[a, mask],
            (me, 1 - rep),
        )
        copy.start()
        started.append(copy)

    def to_partner(a, mask, bit):
        place = fulls[a].at[flip(me, mask), rep]
        got = mask ^ bit
        copy = remote(
            sources[a] if mask == 0 else place, place, ag_send.at[a, got], ag_recv.at[a, got],
            (flip(me, bit), rep),
        )
        copy.start()
        started.append(copy)

    def arrived(a, mask):
        place = fulls[a].at[flip(me, mask), rep]
        remote(
            place, place, ag_send.at[a, mask], ag_recv.at[a, mask], (me, 1 - rep)
        ).wait_recv()

    steps = len(orders[0])
    distances = order_of(n)
    share = -(-len(distances) // max(1, steps))
    held = [[0], [0]]
    for step in range(steps):
        for a in range(2):
            for mask in held[a]:
                to_partner(a, mask, 1 << orders[a][step])
        if step == 0:
            for a in range(2):
                waits.append(pltpu.make_async_copy(sources[a], fulls[a].at[me, rep], own.at[a]))
                waits[-1].start()
                to_sibling(a, 0)
            spread.start_own()
        for d in distances[step * share : (step + 1) * share]:
            spread.start_to(d)
        for a in range(2):
            fresh = [mask ^ (1 << orders[a][step]) for mask in held[a]]
            for mask in fresh:
                arrived(a, mask)
                to_sibling(a, mask)
            held[a] = held[a] + fresh
    for d in distances:
        spread.pass_on(d)
    for a in range(2):
        for mask in range(n):
            place = fulls[a].at[flip(me, mask), 1 - rep]
            remote(
                place, place, sib_send.at[a, mask], sib_recv.at[a, mask], (me, 1 - rep)
            ).wait_recv()
    for copy in waits:
        copy.wait()
    for copy in started:
        copy.wait_send()
    spread.finish()


def spread_kernel(n, src, dst, *sems):
    me, rep = lax.axis_index("dp"), lax.axis_index("rep")
    greet(me, rep, (), n)
    spread = Spread(n, me, rep, src, dst, sems)
    for d in order_of(n):
        spread.start_to(d)
    spread.start_own()
    for d in order_of(n):
        spread.pass_on(d)
    spread.finish()


def return_kernel(n, first, second, out_first, out_second, theirs, mine, *sems):
    me, rep = lax.axis_index("dp"), lax.axis_index("rep")
    greet(me, rep, (), n)
    sib_send, sib_recv, send, recv, local = sems
    started = []
    parts, outs = (first, second), (out_first, out_second)
    distances = order_of(n) + [0]
    for a in range(2):
        for d in distances:
            to = lax.rem(me + d, n)
            copy = remote(
                parts[a].at[1 - rep, to], theirs.at[a, to], sib_send.at[a, d], sib_recv.at[a, d],
                (me, 1 - rep),
            )
            copy.start()
            started.append(copy)
    own = []
    for a in range(2):
        for d in distances:
            to = lax.rem(me + d, n)
            block = theirs.at[a, to]
            remote(
                block, block, sib_send.at[a, d], sib_recv.at[a, d], (me, 1 - rep)
            ).wait_recv()
            mine[a, to] = (
                parts[a][rep, to].astype(jnp.float32) + theirs[a, to].astype(jnp.float32)
            ).astype(jnp.bfloat16)
            if d:
                copy = remote(
                    mine.at[a, to], outs[a].at[me], send.at[a, d], recv.at[a, d], (to, rep)
                )
                copy.start()
                started.append(copy)
            else:
                copy = pltpu.make_async_copy(mine.at[a, me], outs[a].at[me], local.at[a])
                copy.start()
                own.append(copy)
    for copy in own:
        copy.wait()
    for a in range(2):
        for d in order_of(n):
            block = outs[a].at[lax.rem(me + (n - d), n)]
            remote(block, block, send.at[a, d], recv.at[a, d], (me, 1 - rep)).wait_recv()
    for copy in started:
        copy.wait_send()


def reduce_kernel(
    n, cross_ref, gate_ref, bias_ref, cross_out, gate_out, bias_out,
    total, theirs, landed, bias_sum, bias_landed, *sems
):
    me, rep = lax.axis_index("dp"), lax.axis_index("rep")
    steps = n.bit_length() - 1
    greet(me, rep, [1 << b for b in range(steps)])
    sib_send, sib_recv, rs_send, rs_recv, ag_send, ag_recv, b_send, b_recv, own = sems
    parts, outs, orders = (cross_ref, gate_ref), (cross_out, gate_out), bit_orders(n)
    started = []
    f32, bf16 = jnp.float32, jnp.bfloat16

    def send_bias(step, to):
        copy = remote(
            bias_sum.at[step], bias_landed.at[step], b_send.at[step], b_recv.at[step], to
        )
        copy.start()
        started.append(copy)

    def take_bias(step):
        block = bias_landed.at[step]
        remote(block, block, b_send.at[step], b_recv.at[step], (me, 1 - rep)).wait_recv()
        bias_sum[step + 1] = bias_sum[step] + bias_landed[step]

    bias_sum[0] = bias_ref[...]
    send_bias(0, (me, 1 - rep))

    slot_of = [{}, {}]
    for a in range(2):
        masks = list(range(n))
        for step, b in enumerate(orders[a][::-1]):
            masks = [m for m in masks if not m & (1 << b)]
            for m in masks:
                slot_of[a][step, m] = len(slot_of[a])

    def halve(a, step, mask):
        bit = 1 << orders[a][::-1][step]
        at = flip(me, mask)
        slot = slot_of[a][step, mask ^ bit]
        copy = remote(
            total.at[a, at], landed.at[a, slot], rs_send.at[a, slot], rs_recv.at[a, slot],
            (flip(me, bit), rep),
        )
        copy.start()
        started.append(copy)

    def sending_first(a, step, masks):
        if step >= steps:
            return masks
        bit = 1 << orders[a][::-1][step]
        return [m for m in masks if m & bit] + [m for m in masks if not m & bit]

    def maybe_send(a, step, mask):
        if step < steps and mask & (1 << orders[a][::-1][step]):
            halve(a, step, mask)

    todo = [sending_first(a, 0, list(range(n))) for a in range(2)]
    for i in range(n):
        for a in range(2):
            mask = todo[a][i]
            at = flip(me, mask)
            copy = remote(
                parts[a].at[1 - rep, at], theirs.at[a, at], sib_send.at[a, mask],
                sib_recv.at[a, mask], (me, 1 - rep),
            )
            copy.start()
            started.append(copy)
    for i in range(n):
        for a in range(2):
            mask = todo[a][i]
            at = flip(me, mask)
            block = theirs.at[a, at]
            remote(
                block, block, sib_send.at[a, mask], sib_recv.at[a, mask], (me, 1 - rep)
            ).wait_recv()
            total[a, at] = (parts[a][rep, at].astype(f32) + theirs[a, at].astype(f32)).astype(bf16)
            maybe_send(a, 0, mask)
    take_bias(0)

    masks = [list(range(n)), list(range(n))]
    for step in range(steps):
        send_bias(step + 1, (flip(me, 1 << step), rep))
        for a in range(2):
            bit = 1 << orders[a][::-1][step]
            masks[a] = [m for m in masks[a] if not m & bit]
            todo[a] = sending_first(a, step + 1, masks[a])
        for i in range(len(todo[0])):
            for a in range(2):
                mask = todo[a][i]
                at, slot = flip(me, mask), slot_of[a][step, mask]
                block = landed.at[a, slot]
                remote(
                    block, block, rs_send.at[a, slot], rs_recv.at[a, slot], (me, 1 - rep)
                ).wait_recv()
                total[a, at] = (total[a, at].astype(f32) + landed[a, slot].astype(f32)).astype(bf16)
                maybe_send(a, step + 1, mask)
        take_bias(step + 1)
    bias_out[...] = bias_sum[steps + 1]

    held = [[0], [0]]
    waits = []
    for step in range(steps):
        for i in range(len(held[0])):
            for a in range(2):
                mask, bit = held[a][i], 1 << orders[a][step]
                place = outs[a].at[flip(me, mask)]
                copy = remote(
                    total.at[a, me] if mask == 0 else place, place, ag_send.at[a, mask ^ bit],
                    ag_recv.at[a, mask ^ bit], (flip(me, bit), rep),
                )
                copy.start()
                started.append(copy)
        if step == 0:
            for a in range(2):
                waits.append(pltpu.make_async_copy(total.at[a, me], outs[a].at[me], own.at[a]))
                waits[-1].start()
        for a in range(2):
            fresh = [mask ^ (1 << orders[a][step]) for mask in held[a]]
            for mask in fresh:
                place = outs[a].at[flip(me, mask)]
                remote(
                    place, place, ag_send.at[a, mask], ag_recv.at[a, mask], (me, 1 - rep)
                ).wait_recv()
            held[a] = held[a] + fresh
    for copy in waits:
        copy.wait()
    for copy in started:
        copy.wait_send()


ANY = pl.BlockSpec(memory_space=pl.ANY)
VMEM = pl.BlockSpec(memory_space=pltpu.VMEM)


def shape(dims, dtype=jnp.bfloat16):
    return jax.ShapeDtypeStruct(tuple(dims), dtype)


def params(number):
    return pltpu.CompilerParams(
        collective_id=number, has_side_effects=True, vmem_limit_bytes=40 * 1024 * 1024
    )


def body(
    features,
    cotangent,
    routes,
    route_weights,
    counts,
    cross_weight,
    gate_weight,
    cross_bias,
    gate_bias,
    expert_in,
    expert_out,
):
    f32, bf16 = jnp.float32, jnp.bfloat16
    row_count, width = features.shape
    n = lax.axis_size("dp")
    capacity = max(2, 3 * row_count // n)
    slots_n = n * capacity
    shard_rows = cross_weight.shape[0]
    feature_f = features.astype(f32)

    flat_routes = routes.reshape(-1)
    onehot = (flat_routes[:, None] == jnp.arange(n, dtype=jnp.int32)[None, :]).astype(bf16)
    pairs = jnp.arange(2 * row_count, dtype=jnp.int32)
    earlier = (pairs[:, None] > pairs[None, :]).astype(bf16)
    before = jnp.dot(earlier, onehot, preferred_element_type=f32)
    position = jnp.sum(before * onehot.astype(f32), axis=1).astype(jnp.int32)
    slot_index = (flat_routes * capacity + position).reshape(row_count, 2)
    slot_ids = jnp.arange(slots_n, dtype=jnp.int32)
    match = [(slot_index[:, k, None] == slot_ids[None, :]).astype(bf16) for k in range(2)]

    upstream = 0.05 * counts.astype(f32)[:, None] * cotangent.astype(f32)
    both_match = jnp.concatenate(match, axis=0)
    both_grad = jnp.concatenate(
        [(route_weights[:, k, None] * upstream).astype(bf16) for k in range(2)], axis=0
    )

    def to_slots(matches, rows):
        return (
            lax.dot_general(matches, rows, (((0,), (0,)), ((), ())), preferred_element_type=f32)
            .astype(bf16)
            .reshape(n, capacity, width)
        )

    grad_send = to_slots(both_match, both_grad)
    spread_sems = [DMA((n,)), DMA((n,)), DMA((n,)), DMA((n,)), DMA((1,))]
    cross_full, gate_full, slot_grads = pl.pallas_call(
        functools.partial(gather_kernel, n),
        out_shape=(
            shape((n, 2, shard_rows, width)),
            shape((n, 2, shard_rows, width)),
            shape((2, n, capacity, width)),
        ),
        in_specs=[ANY] * 3,
        out_specs=(ANY,) * 3,
        scratch_shapes=[DMA((2, n)), DMA((2, n)), DMA((2, n)), DMA((2, n)), DMA((2,))]
        + spread_sems,
        compiler_params=params(1),
    )(cross_weight, gate_weight, grad_send)

    cross_term = jnp.dot(features, cross_full.reshape(-1, width), preferred_element_type=f32) + cross_bias
    gate_term = jax.nn.sigmoid(
        jnp.dot(features, gate_full.reshape(-1, width), preferred_element_type=f32) + gate_bias
    )
    crossed = (feature_f * cross_term * gate_term + feature_f).astype(bf16)
    row_send = to_slots(match[0] + match[1], crossed)
    slot_rows = pl.pallas_call(
        functools.partial(spread_kernel, n),
        out_shape=shape((2, n, capacity, width)),
        in_specs=[ANY],
        out_specs=ANY,
        scratch_shapes=spread_sems,
        compiler_params=params(2),
    )(row_send)

    rows2 = slot_rows.reshape(2 * slots_n, width)
    grads2 = slot_grads.reshape(2 * slots_n, width)
    weight_in, weight_out = expert_in[0], expert_out[0]
    pre_act = jnp.dot(rows2, weight_in, preferred_element_type=f32)
    squash = jax.nn.sigmoid(pre_act)
    hidden = (pre_act * squash).astype(bf16)
    partial_value = jnp.dot(hidden, weight_out, preferred_element_type=f32).astype(bf16)
    hid_grad = lax.dot_general(
        grads2, weight_out, (((1,), (1,)), ((), ())), preferred_element_type=f32
    )
    pre_grad = (hid_grad * (squash * (1.0 + pre_act * (1.0 - squash)))).astype(bf16)
    back_part = lax.dot_general(
        pre_grad, weight_in, (((1,), (1,)), ((), ())), preferred_element_type=f32
    ).astype(bf16)
    grad_expert_in = lax.dot_general(
        rows2, pre_grad, (((0,), (0,)), ((), ())), preferred_element_type=f32
    ).astype(bf16)[None]
    grad_expert_out = lax.dot_general(
        hidden, grads2, (((0,), (0,)), ((), ())), preferred_element_type=f32
    ).astype(bf16)[None]

    blocks = (2, n, capacity, width)
    back, returned = pl.pallas_call(
        functools.partial(return_kernel, n),
        out_shape=(shape(blocks[1:]),) * 2,
        in_specs=[VMEM] * 2,
        out_specs=(ANY,) * 2,
        scratch_shapes=[pltpu.VMEM(blocks, bf16), pltpu.VMEM(blocks, bf16)]
        + [DMA((2, n))] * 4
        + [DMA((2,))],
        compiler_params=params(3),
    )(back_part.reshape(blocks), partial_value.reshape(blocks))

    def of_row(k, values):
        return jnp.dot(match[k], values.reshape(slots_n, width), preferred_element_type=f32)

    layer_output = (
        crossed.astype(f32)
        + route_weights[:, 0, None] * of_row(0, returned)
        + route_weights[:, 1, None] * of_row(1, returned)
    ).astype(bf16)
    crossed_grad = upstream + of_row(0, back) + of_row(1, back)
    cross_grad = (crossed_grad * feature_f * gate_term).astype(bf16)
    gate_grad = (crossed_grad * feature_f * cross_term * gate_term * (1.0 - gate_term)).astype(bf16)

    def weight_sum(values):
        return (
            lax.dot_general(features, values, (((0,), (0,)), ((), ())), preferred_element_type=f32)
            .astype(bf16)
            .reshape(2, n, -1, width)
        )

    sums = (weight_sum(cross_grad), weight_sum(gate_grad))
    biases = jnp.stack(
        [jnp.sum(cross_grad.astype(f32), axis=0), jnp.sum(gate_grad.astype(f32), axis=0)]
    )
    biases = jnp.concatenate([biases, jnp.zeros((6, width), f32)], axis=0)
    part = sums[0].shape[2]
    steps = n.bit_length() - 1
    grad_cross, grad_gate, bias_total = pl.pallas_call(
        functools.partial(reduce_kernel, n),
        out_shape=(shape((n, part, width)), shape((n, part, width)), shape((8, width), f32)),
        in_specs=[VMEM] * 3,
        out_specs=(ANY, ANY, VMEM),
        scratch_shapes=[
            pltpu.VMEM((2, n, part, width), bf16),
            pltpu.VMEM((2, n, part, width), bf16),
            pltpu.VMEM((2, n, part, width), bf16),
            pltpu.VMEM((steps + 2, 8, width), f32),
            pltpu.VMEM((steps + 1, 8, width), f32),
        ]
        + [DMA((2, n))] * 6
        + [DMA((steps + 1,))] * 2
        + [DMA((2,))],
        compiler_params=params(4),
    )(*sums, biases)
    half = width // 2
    start = lax.axis_index("rep") * half
    bias_half = lax.dynamic_slice_in_dim(bias_total, start, half, axis=1)
    return (
        layer_output,
        grad_cross.reshape(-1, width),
        grad_gate.reshape(-1, width),
        bias_half[0],
        bias_half[1],
        grad_expert_in,
        grad_expert_out,
    )


def solution(mesh):
    return jax.shard_map(
        body,
        mesh=mesh,
        in_specs=(
            P(("dp", "rep"), None),
            P(("dp", "rep"), None),
            P(("dp", "rep"), None),
            P(("dp", "rep"), None),
            P(("dp", "rep")),
            P(("dp", "rep"), None),
            P(("dp", "rep"), None),
            P(),
            P(),
            P("dp", None, "rep"),
            P("dp", "rep", None),
        ),
        out_specs=(
            P(("dp", "rep"), None),
            P("rep", None),
            P("rep", None),
            P("rep"),
            P("rep"),
            P("dp", None, "rep"),
            P("dp", "rep", None),
        ),
        check_vma=False,
    )
```

time: 415 us -> 210 us (0.51)
  waiting for transfers between devices: 247 us -> 0 us
  Pallas kernels: 0 us -> 182 us
  blocking collectives: 69 us -> 0 us
  matrix products: 40.6 us -> 20 us
  starting transfers between devices: 16.6 us -> 0 us
  local copies, waits for them, and re-layouts: 19.1 us -> 4.6 us
  between operations: 14.8 us -> 0.92 us
  other arithmetic: 7.01 us -> 2.83 us
    pallas_call x0 -> x4, Pallas kernels: none -> 182 us  [the longest x1 70.2 us: body(): pl.pallas_call(functools.partial(reduce_kernel, n), out_shape=(shape((n,...]
    all_gather x4 -> x0, waiting for transfers between devices: 118 us -> none  [the longest x1 59 us: body(): lax.all_gather(cross_weight, ('dp', 'rep'), axis=0, tiled=True)]
    psum x1 -> x0, waiting for transfers between devices: 73.9 us -> none  [body(): summed = lax.psum((halves[0], halves[1], halves[2], halves[3]), 'dp')]
    psum x1 -> x0, blocking collectives: 41.3 us -> none  [body(): summed = lax.psum((halves[0], halves[1], halves[2], halves[3]), 'dp')]
    all_to_all x3 -> x0, waiting for transfers between devices: 40.4 us -> none  [the longest x1 19.7 us: body(): lax.all_to_all(back_rows, 'dp', split_axis=0, concat_axis=0, tiled=True)]
    all_to_all x1 -> x0, blocking collectives: 25.2 us -> none  [body(): lax.all_to_all(grad_send, 'dp', split_axis=0, concat_axis=0, tiled=True)]
    dot_general x12 -> x17, matrix products: 40.6 us -> 20 us  [the longest x1 3.24 us: body(): lax.dot_general(hidden, grads2, (((0,), (0,)), ((), ())), preferred_eleme...]
    all_to_all x3 -> x0, starting transfers between devices: 16 us -> none  [the longest x1 6.83 us: body(): lax.all_to_all(back_rows, 'dp', split_axis=0, concat_axis=0, tiled=True)]
  transfers between devices with their start and end apart: 12 -> 0, of which waited for: 9 -> 0; matrix products, arithmetic and copies ran while one was open for 12% -> 0% of each run, Pallas kernels for 0% -> 0%
where the time goes in v1:
time: 210 us
  Pallas kernels  182 us (87%)
  matrix products  20 us (10%)
  local copies, waits for them, and re-layouts  4.6 us (2%)
  other arithmetic  2.83 us (1%)
    pallas_call x1, Pallas kernels, body(): pl.pallas_call(functools.partial(reduce_kernel, n), out_shape=(shape((n,...  70.2 us
    pallas_call x1, Pallas kernels, body(): pl.pallas_call(functools.partial(gather_kernel, n), out_shape=(shape((n,...  51.8 us
    pallas_call x1, Pallas kernels, body(): pl.pallas_call(functools.partial(return_kernel, n), out_shape=(shape(bloc...  41.6 us
    pallas_call x1, Pallas kernels, body(): pl.pallas_call(functools.partial(spread_kernel, n), out_shape=shape((2, n...  18 us

profile of v1, /device:TPU:0, one launch (start us, length us, event | category | flops | bytes accessed | tf_op | source)
XLA Modules:
  0.0 209.9 jit_solution(9315416282997053608)
XLA Ops:
  0.6 0.0 copy-start
  0.6 0.0 copy-start.3
  0.7 0.0 copy-start.5
  0.7 0.0 copy-start.2
  0.7 0.0 copy-start.1
  0.7 0.8 convert_multiply_fusion.2
  1.5 0.1 pad.2.clone
  1.6 0.8 slice_bitcast_fusion.1
  2.3 0.8 copy.24
  3.1 0.1 eq.45
  3.3 0.2 fusion.26
  3.5 0.1 convert_element_type.96
  3.6 0.1 copy.25
  3.7 0.7 multiply_add_fusion
  4.4 0.1 fusion.35
  4.5 1.1 multiply_convert_fusion.5
  5.6 0.4 convolution_convert_fusion.3
  6.0 0.0 copy-start.7
  6.1 0.0 copy-done.2
  6.1 0.0 copy-done.1
  6.1 51.8 %shard_map.162 = (bf16[16,2,32,1024]{3,2,1,0:T(8,128)(2,1)S(1)}, bf16[16,2,32,1024]{3,2,1,0:T(8,128)(2,1)S(1)}, bf16[2,16,24,1024]{3,2,1,0:T(8,128)(2,1)S(1)}) custom-call(bf16[32,1024]{1,0:T(8,128)(2,1)S(1)} %copy-done.1, bf16[32,1024]{1,0:T(8,128)(2,1)S(1)} %copy-done.2, bf16[16,24,1024]{2,1,0:T(8,128)(2,1)S(1)} %bitcast.87), custom_call_target="tpu_custom_call" | custom-call | tf_op jit(solution)/shard_map/pallas_call | solution.py:428
  57.9 0.0 copy-done.3
  57.9 0.0 copy-done.5
  57.9 0.4 fusion.21
  58.3 0.0 copy-done.7
  58.3 0.5 fusion.28
  58.9 0.0 copy-start.6
  58.9 0.5 convolution_convert_fusion.2
  59.4 18.0 %shard_map.163 = bf16[2,16,24,1024]{3,2,1,0:T(8,128)(2,1)S(1)} custom-call(bf16[16,24,1024]{2,1,0:T(8,128)(2,1)S(1)} %bitcast.75), custom_call_target="tpu_custom_call" | custom-call | tf_op jit(solution)/shard_map/pallas_call | solution.py:448
  77.4 0.0 copy-done.6
  77.4 1.8 fusion.2
  79.2 0.0 copy-done
  79.2 2.4 %multiply_convert_fusion.1 = bf16[768,1024]{1,0:T(8,128)(2,1)S(1)} fusion(f32[768,1024]{1,0:T(8,128)S(1)} %fusion.2, bf16[768,1024]{1,0:T(8,128)(2,1)S(1)} %bitcast.89, bf16[1,1024,1024]{2,1,0:T(8,128)(2,1)S(1)} %copy-done), kind=kOutput, calls=%fused_computation.1 | convolution fusion | flops 1617690624 | bytes 8388608 | tf_op jit(solution)/shard_map/dot_general | solution.py:464
  81.6 3.2 %convert_bitcast_fusion = bf16[1,1024,1024]{2,1,0:T(8,128)(2,1)} fusion(bf16[768,1024]{1,0:T(8,128)(2,1)S(1)} %bitcast.90, f32[768,1024]{1,0:T(8,128)S(1)} %fusion.2), kind=kOutput, calls=%fused_computation.11 | convolution fusion | flops 1615593472 | bytes 6815744 | tf_op jit(solution)/shard_map/dot_general | solution.py:474
  84.8 1.8 fusion.8
  86.7 3.2 %convert_bitcast_fusion.1 = bf16[1,1024,1024]{2,1,0:T(8,128)(2,1)} fusion(bf16[768,1024]{1,0:T(8,128)(2,1)S(1)} %bitcast.82, bf16[768,1024]{1,0:T(8,128)(2,1)S(1)} %multiply_convert_fusion.1), kind=kOutput, calls=%fused_computation.12 | convolution fusion | flops 1611661312 | bytes 5242880 | tf_op jit(solution)/shard_map/dot_general | solution.py:471
  89.9 1.8 fusion.11
  91.7 41.6 %shard_map.164 = (bf16[16,24,1024]{2,1,0:T(8,128)(2,1)S(1)}, bf16[16,24,1024]{2,1,0:T(8,128)(2,1)S(1)}) custom-call(bf16[2,16,24,1024]{3,2,1,0:T(8,128)(2,1)S(1)} %bitcast.84, bf16[2,16,24,1024]{3,2,1,0:T(8,128)(2,1)S(1)} %bitcast.83), custom_call_target="tpu_custom_call" | custom-call | tf_op jit(solution)/shard_map/pallas_call | solution.py:479
  133.3 0.0 copy-start.4
  133.3 0.4 fusion.24
  133.6 1.1 fusion.25
  134.7 0.0 copy-done.4
  134.7 0.3 convolution_add_fusion.3
  135.1 0.4 convert_reduce_fusion
  135.5 0.1 maximum_maximum_fusion.bias_ref
  135.6 0.7 convolution_convert_fusion
  136.3 0.7 convolution_convert_fusion.1
  137.1 70.2 %shard_map.165 = (bf16[16,32,1024]{2,1,0:T(8,128)(2,1)S(1)}, bf16[16,32,1024]{2,1,0:T(8,128)(2,1)S(1)}, f32[8,1024]{1,0:T(8,128)S(1)}) custom-call(bf16[2,16,32,1024]{3,2,1,0:T(8,128)(2,1)S(1)} %bitcast.74, bf16[2,16,32,1024]{3,2,1,0:T(8,128)(2,1)S(1)} %bitcast.73, f32[8,1024]{1,0:T(8,128)S(1)} %maximum_maximum_fusion.bias_ref), custom_call_target="tpu_custom_call" | custom-call | tf_op jit(solution)/shard_map/pallas_call | solution.py:516
  207.3 0.7 fusion.47
  208.0 1.0 copy.28
  208.9 1.0 copy.29
  (3 shorter events, 0.0 us)
Async XLA Ops:
  0.6 78.6 %copy-start = (bf16[1,1024,1024]{2,1,0:T(8,128)(2,1)S(1)}, bf16[1,1024,1024]{2,1,0:T(8,128)(2,1)}, u32[]{:S(2)}) copy-start(bf16[1,1024,1024]{2,1,0:T(8,128)(2,1)} %param.21) | copy-start | bytes 6291460
  0.6 57.2 %copy-start.3 = (bf16[128,1024]{1,0:T(8,128)(2,1)S(1)}, bf16[128,1024]{1,0:T(8,128)(2,1)}, u32[]{:S(2)}) copy-start(bf16[128,1024]{1,0:T(8,128)(2,1)} %param.11) | copy-start | bytes 786436
  0.7 57.2 %copy-start.5 = (f32[1024]{0:T(1024)S(1)}, f32[1024]{0:T(1024)}, u32[]{:S(2)}) copy-start(f32[1024]{0:T(1024)} %param.18) | copy-start | bytes 12292
  0.7 5.4 %copy-start.2 = (bf16[32,1024]{1,0:T(8,128)(2,1)S(1)}, bf16[32,1024]{1,0:T(8,128)(2,1)}, u32[]{:S(2)}) copy-start(bf16[32,1024]{1,0:T(8,128)(2,1)} %gate_ref.1) | copy-start | bytes 196612
  0.7 5.4 %copy-start.1 = (bf16[32,1024]{1,0:T(8,128)(2,1)S(1)}, bf16[32,1024]{1,0:T(8,128)(2,1)}, u32[]{:S(2)}) copy-start(bf16[32,1024]{1,0:T(8,128)(2,1)} %cross_ref.1) | copy-start | bytes 196612
  6.0 52.3 %copy-start.7 = (f32[1024]{0:T(1024)S(1)}, f32[1024]{0:T(1024)}, u32[]{:S(2)}) copy-start(f32[1024]{0:T(1024)} %param.19) | copy-start | bytes 12292
  58.9 18.5 %copy-start.6 = (bf16[1,1024,1024]{2,1,0:T(8,128)(2,1)S(1)}, bf16[1,1024,1024]{2,1,0:T(8,128)(2,1)}, u32[]{:S(2)}) copy-start(bf16[1,1024,1024]{2,1,0:T(8,128)(2,1)} %param.20) | copy-start | bytes 6291460
  133.3 1.4 copy-start.4

commit v2 on v1

--- a/solution.py
+++ b/solution.py
@@ -20,11 +20,22 @@
     return index
 
 
-def bit_orders(n):
+def stream_count(rows, width):
+    return 6 if rows * width >= 16 * 1024 and width >= 384 else 2
+
+
+def streams_of(n, streams, width):
     bits = n.bit_length() - 1
-    down = list(range(bits))[::-1]
-    turned = down[:1] + down[2:] + down[1:2]
-    return down, turned
+    first, rest = list(range(bits))[::-1][:1], list(range(bits))[::-1][1:]
+    pieces = streams // 2
+    edges = [-(-width // 128 * p // pieces) * 128 for p in range(pieces)] + [width]
+    found = []
+    for p in range(pieces):
+        for a in range(2):
+            turn = (p if pieces > 1 else a) % max(1, len(rest))
+            columns = slice(edges[p], edges[p + 1])
+            found.append((a, columns, first + rest[turn:] + rest[:turn]))
+    return found
 
 
 def greet(me, rep, partners, everyone=0):
@@ -111,30 +122,40 @@
     greet(me, rep, (), n)
     spread = Spread(n, me, rep, grads_ref, slots, sems[5:])
     ag_send, ag_recv, sib_send, sib_recv, own = sems[:5]
-    sources, fulls, orders = (cross_ref, gate_ref), (cross_full, gate_full), bit_orders(n)
+    sources, fulls = (cross_ref, gate_ref), (cross_full, gate_full)
+    plan = streams_of(n, stream_count(*cross_ref.shape), cross_ref.shape[1])
+    orders = [order for _, _, order in plan]
     started, waits = [], []
 
+    def source(q):
+        a, columns, _ = plan[q]
+        return sources[a].at[:, columns]
+
+    def full(q, row, core):
+        a, columns, _ = plan[q]
+        return fulls[a].at[row, core, :, columns]
+
     def to_sibling(a, mask):
-        place = fulls[a].at[flip(me, mask), rep]
+        place = full(a, flip(me, mask), rep)
         copy = remote(
-            sources[a] if mask == 0 else place, place, sib_send.at[a, mask], sib_recv.at[a, mask],
+            source(a) if mask == 0 else place, place, sib_send.at[a, mask], sib_recv.at[a, mask],
             (me, 1 - rep),
         )
         copy.start()
         started.append(copy)
 
     def to_partner(a, mask, bit):
-        place = fulls[a].at[flip(me, mask), rep]
+        place = full(a, flip(me, mask), rep)
         got = mask ^ bit
         copy = remote(
-            sources[a] if mask == 0 else place, place, ag_send.at[a, got], ag_recv.at[a, got],
+            source(a) if mask == 0 else place, place, ag_send.at[a, got], ag_recv.at[a, got],
             (flip(me, bit), rep),
         )
         copy.start()
         started.append(copy)
 
     def arrived(a, mask):
-        place = fulls[a].at[flip(me, mask), rep]
+        place = full(a, flip(me, mask), rep)
         remote(
             place, place, ag_send.at[a, mask], ag_recv.at[a, mask], (me, 1 - rep)
         ).wait_recv()
@@ -142,20 +163,21 @@
     steps = len(orders[0])
     distances = order_of(n)
     share = -(-len(distances) // max(1, steps))
-    held = [[0], [0]]
+    held = [[0] for _ in plan]
     for step in range(steps):
-        for a in range(2):
+        for a in range(len(plan)):
             for mask in held[a]:
                 to_partner(a, mask, 1 << orders[a][step])
         if step == 0:
             for a in range(2):
                 waits.append(pltpu.make_async_copy(sources[a], fulls[a].at[me, rep], own.at[a]))
                 waits[-1].start()
+            for a in range(len(plan)):
                 to_sibling(a, 0)
             spread.start_own()
         for d in distances[step * share : (step + 1) * share]:
             spread.start_to(d)
-        for a in range(2):
+        for a in range(len(plan)):
             fresh = [mask ^ (1 << orders[a][step]) for mask in held[a]]
             for mask in fresh:
                 arrived(a, mask)
@@ -163,9 +185,9 @@
             held[a] = held[a] + fresh
     for d in distances:
         spread.pass_on(d)
-    for a in range(2):
+    for a in range(len(plan)):
         for mask in range(n):
-            place = fulls[a].at[flip(me, mask), 1 - rep]
+            place = full(a, flip(me, mask), 1 - rep)
             remote(
                 place, place, sib_send.at[a, mask], sib_recv.at[a, mask], (me, 1 - rep)
             ).wait_recv()
@@ -243,8 +265,23 @@
     steps = n.bit_length() - 1
     greet(me, rep, [1 << b for b in range(steps)])
     sib_send, sib_recv, rs_send, rs_recv, ag_send, ag_recv, b_send, b_recv, own = sems
-    parts, outs, orders = (cross_ref, gate_ref), (cross_out, gate_out), bit_orders(n)
+    parts, outs = (cross_ref, gate_ref), (cross_out, gate_out)
+    plan = streams_of(n, stream_count(*cross_ref.shape[2:]), cross_ref.shape[3])
+    orders = [order for _, _, order in plan]
+    many = range(len(plan))
     started = []
+
+    def held_at(q, row):
+        a, columns, _ = plan[q]
+        return total.at[a, row, :, columns]
+
+    def landed_at(q, slot):
+        a, columns, _ = plan[q]
+        return landed.at[a, slot, :, columns]
+
+    def out_at(q, row):
+        a, columns, _ = plan[q]
+        return outs[a].at[row, :, columns]
     f32, bf16 = jnp.float32, jnp.bfloat16
 
     def send_bias(step, to):
@@ -262,8 +299,8 @@
     bias_sum[0] = bias_ref[...]
     send_bias(0, (me, 1 - rep))
 
-    slot_of = [{}, {}]
-    for a in range(2):
+    slot_of = [{} for _ in many]
+    for a in many:
         masks = list(range(n))
         for step, b in enumerate(orders[a][::-1]):
             masks = [m for m in masks if not m & (1 << b)]
@@ -275,7 +312,7 @@
         at = flip(me, mask)
         slot = slot_of[a][step, mask ^ bit]
         copy = remote(
-            total.at[a, at], landed.at[a, slot], rs_send.at[a, slot], rs_recv.at[a, slot],
+            held_at(a, at), landed_at(a, slot), rs_send.at[a, slot], rs_recv.at[a, slot],
             (flip(me, bit), rep),
         )
         copy.start()
@@ -291,10 +328,8 @@
         if step < steps and mask & (1 << orders[a][::-1][step]):
             halve(a, step, mask)
 
-    todo = [sending_first(a, 0, list(range(n))) for a in range(2)]
-    for i in range(n):
+    for mask in reversed(range(n)):
         for a in range(2):
-            mask = todo[a][i]
             at = flip(me, mask)
             copy = remote(
                 parts[a].at[1 - rep, at], theirs.at[a, at], sib_send.at[a, mask],
@@ -302,47 +337,50 @@
             )
             copy.start()
             started.append(copy)
-    for i in range(n):
+    for mask in reversed(range(n)):
+        at = flip(me, mask)
         for a in range(2):
-            mask = todo[a][i]
-            at = flip(me, mask)
             block = theirs.at[a, at]
             remote(
                 block, block, sib_send.at[a, mask], sib_recv.at[a, mask], (me, 1 - rep)
             ).wait_recv()
             total[a, at] = (parts[a][rep, at].astype(f32) + theirs[a, at].astype(f32)).astype(bf16)
-            maybe_send(a, 0, mask)
+            for q in many:
+                if plan[q][0] == a:
+                    maybe_send(q, 0, mask)
     take_bias(0)
 
-    masks = [list(range(n)), list(range(n))]
+    masks = [list(range(n)) for _ in many]
+    todo = [None for _ in many]
     for step in range(steps):
         send_bias(step + 1, (flip(me, 1 << step), rep))
-        for a in range(2):
+        for a in many:
             bit = 1 << orders[a][::-1][step]
             masks[a] = [m for m in masks[a] if not m & bit]
             todo[a] = sending_first(a, step + 1, masks[a])
         for i in range(len(todo[0])):
-            for a in range(2):
+            for a in many:
                 mask = todo[a][i]
                 at, slot = flip(me, mask), slot_of[a][step, mask]
-                block = landed.at[a, slot]
+                block = landed_at(a, slot)
                 remote(
                     block, block, rs_send.at[a, slot], rs_recv.at[a, slot], (me, 1 - rep)
                 ).wait_recv()
-                total[a, at] = (total[a, at].astype(f32) + landed[a, slot].astype(f32)).astype(bf16)
+                into = held_at(a, at)
+                into[...] = (into[...].astype(f32) + block[...].astype(f32)).astype(bf16)
                 maybe_send(a, step + 1, mask)
         take_bias(step + 1)
     bias_out[...] = bias_sum[steps + 1]
 
-    held = [[0], [0]]
+    held = [[0] for _ in many]
     waits = []
     for step in range(steps):
         for i in range(len(held[0])):
-            for a in range(2):
+            for a in many:
                 mask, bit = held[a][i], 1 << orders[a][step]
-                place = outs[a].at[flip(me, mask)]
+                place = out_at(a, flip(me, mask))
                 copy = remote(
-                    total.at[a, me] if mask == 0 else place, place, ag_send.at[a, mask ^ bit],
+                    held_at(a, me) if mask == 0 else place, place, ag_send.at[a, mask ^ bit],
                     ag_recv.at[a, mask ^ bit], (flip(me, bit), rep),
                 )
                 copy.start()
@@ -351,10 +389,10 @@
             for a in range(2):
                 waits.append(pltpu.make_async_copy(total.at[a, me], outs[a].at[me], own.at[a]))
                 waits[-1].start()
-        for a in range(2):
+        for a in many:
             fresh = [mask ^ (1 << orders[a][step]) for mask in held[a]]
             for mask in fresh:
-                place = outs[a].at[flip(me, mask)]
+                place = out_at(a, flip(me, mask))
                 remote(
                     place, place, ag_send.at[a, mask], ag_recv.at[a, mask], (me, 1 - rep)
                 ).wait_recv()
@@ -434,8 +472,7 @@
         ),
         in_specs=[ANY] * 3,
         out_specs=(ANY,) * 3,
-        scratch_shapes=[DMA((2, n)), DMA((2, n)), DMA((2, n)), DMA((2, n)), DMA((2,))]
-        + spread_sems,
+        scratch_shapes=[DMA((stream_count(shard_rows, width), n))] * 4 + [DMA((2,))] + spread_sems,
         compiler_params=params(1),
     )(cross_weight, gate_weight, grad_send)
 
@@ -525,7 +562,8 @@
             pltpu.VMEM((steps + 2, 8, width), f32),
             pltpu.VMEM((steps + 1, 8, width), f32),
         ]
-        + [DMA((2, n))] * 6
+        + [DMA((2, n))] * 2
+        + [DMA((stream_count(part, width), n))] * 4
         + [DMA((steps + 1,))] * 2
         + [DMA((2,))],
         compiler_params=params(4),

time: 210 us -> 202 us (0.962)
  Pallas kernels: 182 us -> 174 us
    pallas_call x1, Pallas kernels: 70.2 us -> 64.2 us  [body(): pl.pallas_call(functools.partial(reduce_kernel, n), out_shape=(shape((n,...]
    pallas_call x1, Pallas kernels: 51.8 us -> 49.1 us  [body(): pl.pallas_call(functools.partial(gather_kernel, n), out_shape=(shape((n,...]
where the time goes in v2:
time: 202 us
  Pallas kernels  174 us (86%)
  matrix products  20 us (10%)
  local copies, waits for them, and re-layouts  4.6 us (2%)
  other arithmetic  2.83 us (1%)
    pallas_call x1, Pallas kernels, body(): pl.pallas_call(functools.partial(reduce_kernel, n), out_shape=(shape((n,...  64.2 us
    pallas_call x1, Pallas kernels, body(): pl.pallas_call(functools.partial(gather_kernel, n), out_shape=(shape((n,...  49.1 us
    pallas_call x1, Pallas kernels, body(): pl.pallas_call(functools.partial(return_kernel, n), out_shape=(shape(bloc...  41.8 us
    pallas_call x1, Pallas kernels, body(): pl.pallas_call(functools.partial(spread_kernel, n), out_shape=shape((2, n...  18.8 us

profile of v2, /device:TPU:0, one launch (start us, length us, event | category | flops | bytes accessed | tf_op | source)
XLA Modules:
  0.0 202.3 jit_solution(2099358647018458043)
XLA Ops:
  0.6 0.0 copy-start
  0.6 0.0 copy-start.3
  0.7 0.0 copy-start.5
  0.7 0.0 copy-start.2
  0.7 0.0 copy-start.1
  0.7 0.8 convert_multiply_fusion.2
  1.5 0.1 pad.2.clone
  1.6 0.8 slice_bitcast_fusion.1
  2.3 0.8 copy.24
  3.1 0.1 eq.45
  3.3 0.2 fusion.26
  3.5 0.1 convert_element_type.96
  3.6 0.1 copy.25
  3.7 0.7 multiply_add_fusion
  4.4 0.1 fusion.35
  4.5 1.1 multiply_convert_fusion.5
  5.6 0.4 convolution_convert_fusion.3
  6.0 0.0 copy-start.7
  6.1 0.0 copy-done.2
  6.1 0.0 copy-done.1
  6.1 49.1 %shard_map.162 = (bf16[16,2,32,1024]{3,2,1,0:T(8,128)(2,1)S(1)}, bf16[16,2,32,1024]{3,2,1,0:T(8,128)(2,1)S(1)}, bf16[2,16,24,1024]{3,2,1,0:T(8,128)(2,1)S(1)}) custom-call(bf16[32,1024]{1,0:T(8,128)(2,1)S(1)} %copy-done.1, bf16[32,1024]{1,0:T(8,128)(2,1)S(1)} %copy-done.2, bf16[16,24,1024]{2,1,0:T(8,128)(2,1)S(1)} %bitcast.87), custom_call_target="tpu_custom_call" | custom-call | tf_op jit(solution)/shard_map/pallas_call | solution.py:466
  55.2 0.0 copy-done.3
  55.2 0.0 copy-done.5
  55.2 0.4 fusion.21
  55.6 0.0 copy-done.7
  55.6 0.5 fusion.28
  56.2 0.0 copy-start.6
  56.2 0.5 convolution_convert_fusion.2
  56.7 18.8 %shard_map.163 = bf16[2,16,24,1024]{3,2,1,0:T(8,128)(2,1)S(1)} custom-call(bf16[16,24,1024]{2,1,0:T(8,128)(2,1)S(1)} %bitcast.75), custom_call_target="tpu_custom_call" | custom-call | tf_op jit(solution)/shard_map/pallas_call | solution.py:485
  75.5 0.0 copy-done.6
  75.5 1.8 fusion.2
  77.3 0.0 copy-done
  77.3 2.4 %multiply_convert_fusion.1 = bf16[768,1024]{1,0:T(8,128)(2,1)S(1)} fusion(f32[768,1024]{1,0:T(8,128)S(1)} %fusion.2, bf16[768,1024]{1,0:T(8,128)(2,1)S(1)} %bitcast.89, bf16[1,1024,1024]{2,1,0:T(8,128)(2,1)S(1)} %copy-done), kind=kOutput, calls=%fused_computation.1 | convolution fusion | flops 1617690624 | bytes 8388608 | tf_op jit(solution)/shard_map/dot_general | solution.py:501
  79.7 3.2 %convert_bitcast_fusion = bf16[1,1024,1024]{2,1,0:T(8,128)(2,1)} fusion(bf16[768,1024]{1,0:T(8,128)(2,1)S(1)} %bitcast.90, f32[768,1024]{1,0:T(8,128)S(1)} %fusion.2), kind=kOutput, calls=%fused_computation.11 | convolution fusion | flops 1615593472 | bytes 6815744 | tf_op jit(solution)/shard_map/dot_general | solution.py:511
  82.9 1.8 fusion.8
  84.7 3.2 %convert_bitcast_fusion.1 = bf16[1,1024,1024]{2,1,0:T(8,128)(2,1)} fusion(bf16[768,1024]{1,0:T(8,128)(2,1)S(1)} %bitcast.82, bf16[768,1024]{1,0:T(8,128)(2,1)S(1)} %multiply_convert_fusion.1), kind=kOutput, calls=%fused_computation.12 | convolution fusion | flops 1611661312 | bytes 5242880 | tf_op jit(solution)/shard_map/dot_general | solution.py:508
  87.9 1.8 fusion.11
  89.7 41.8 %shard_map.164 = (bf16[16,24,1024]{2,1,0:T(8,128)(2,1)S(1)}, bf16[16,24,1024]{2,1,0:T(8,128)(2,1)S(1)}) custom-call(bf16[2,16,24,1024]{3,2,1,0:T(8,128)(2,1)S(1)} %bitcast.84, bf16[2,16,24,1024]{3,2,1,0:T(8,128)(2,1)S(1)} %bitcast.83), custom_call_target="tpu_custom_call" | custom-call | tf_op jit(solution)/shard_map/pallas_call | solution.py:516
  131.6 0.0 copy-start.4
  131.6 0.4 fusion.24
  132.0 1.1 fusion.25
  133.0 0.0 copy-done.4
  133.0 0.3 convolution_add_fusion.3
  133.4 0.4 convert_reduce_fusion
  133.8 0.1 maximum_maximum_fusion.bias_ref
  133.9 0.7 convolution_convert_fusion
  134.7 0.7 convolution_convert_fusion.1
  135.4 64.2 %shard_map.165 = (bf16[16,32,1024]{2,1,0:T(8,128)(2,1)S(1)}, bf16[16,32,1024]{2,1,0:T(8,128)(2,1)S(1)}, f32[8,1024]{1,0:T(8,128)S(1)}) custom-call(bf16[2,16,32,1024]{3,2,1,0:T(8,128)(2,1)S(1)} %bitcast.74, bf16[2,16,32,1024]{3,2,1,0:T(8,128)(2,1)S(1)} %bitcast.73, f32[8,1024]{1,0:T(8,128)S(1)} %maximum_maximum_fusion.bias_ref), custom_call_target="tpu_custom_call" | custom-call | tf_op jit(solution)/shard_map/pallas_call | solution.py:553
  199.7 0.7 fusion.47
  200.3 1.0 copy.28
  201.3 1.0 copy.29
  (3 shorter events, 0.0 us)
Async XLA Ops:
  0.6 76.6 %copy-start = (bf16[1,1024,1024]{2,1,0:T(8,128)(2,1)S(1)}, bf16[1,1024,1024]{2,1,0:T(8,128)(2,1)}, u32[]{:S(2)}) copy-start(bf16[1,1024,1024]{2,1,0:T(8,128)(2,1)} %param.21) | copy-start | bytes 6291460
  0.6 54.5 %copy-start.3 = (bf16[128,1024]{1,0:T(8,128)(2,1)S(1)}, bf16[128,1024]{1,0:T(8,128)(2,1)}, u32[]{:S(2)}) copy-start(bf16[128,1024]{1,0:T(8,128)(2,1)} %param.11) | copy-start | bytes 786436
  0.7 54.5 %copy-start.5 = (f32[1024]{0:T(1024)S(1)}, f32[1024]{0:T(1024)}, u32[]{:S(2)}) copy-start(f32[1024]{0:T(1024)} %param.18) | copy-start | bytes 12292
  0.7 5.4 %copy-start.2 = (bf16[32,1024]{1,0:T(8,128)(2,1)S(1)}, bf16[32,1024]{1,0:T(8,128)(2,1)}, u32[]{:S(2)}) copy-start(bf16[32,1024]{1,0:T(8,128)(2,1)} %gate_ref.1) | copy-start | bytes 196612
  0.7 5.4 %copy-start.1 = (bf16[32,1024]{1,0:T(8,128)(2,1)S(1)}, bf16[32,1024]{1,0:T(8,128)(2,1)}, u32[]{:S(2)}) copy-start(bf16[32,1024]{1,0:T(8,128)(2,1)} %cross_ref.1) | copy-start | bytes 196612
  6.0 49.6 %copy-start.7 = (f32[1024]{0:T(1024)S(1)}, f32[1024]{0:T(1024)}, u32[]{:S(2)}) copy-start(f32[1024]{0:T(1024)} %param.19) | copy-start | bytes 12292
  56.2 19.3 %copy-start.6 = (bf16[1,1024,1024]{2,1,0:T(8,128)(2,1)S(1)}, bf16[1,1024,1024]{2,1,0:T(8,128)(2,1)}, u32[]{:S(2)}) copy-start(bf16[1,1024,1024]{2,1,0:T(8,128)(2,1)} %param.20) | copy-start | bytes 6291460
  131.6 1.4 copy-start.4
